TPU v7x, 128 devices: a whole 4x4x4 slice. The times are simulated.
128 devices in a mesh: group: 2 (over z_hi), dev: 64 (over x, z_lo, y, core).
Axes of the slice: x: 4, y: 4, z: 4 (z_hi: 2, z_lo: 2; z = z_hi * 2 + z_lo), core: 2. Of those that a mesh axis runs over, the one named last changes fastest.
Arguments:
- new_weights: bfloat16 [64, 3584, 1024], P(None, ('group', 'dev')), may hold values from -80 to 80
- owner_map: int32 [64], replicated, may hold values from 0 to 63, each once
- block_mask: int32 [64, 28, 8], replicated, may hold values from 0 to 1, as said below
- base_codes: bfloat16 [64, 3584, 1024], P('dev'), may hold values from -8 to 7, as said below
- base_scale: float32 [64, 28, 8], P('dev'), may hold values from 0.05 to 0.4
Outputs:
- delta_blocks: bfloat16 [2, 64, 3584, 1024], P('group', 'dev')
- delta_scales: bfloat16 [2, 64, 28, 8], P('group', 'dev')
Inputs may be any that keep to these rules, and one draw needn't show every extreme that they name: `base_codes`: whole numbers. `block_mask`: of each expert, every block row (a fixed a) holds exactly 4 ones.
All inputs are finite; a program needn't handle non-finite values.
Results may differ from a plain program's by a relative error of at most 0.001.
Values may be sent and summed in bfloat16 or wider, within the bound.
A program may use at most 128 MiB of HBM per device.

v0:
```python
import jax
import jax.numpy as jnp
from jax import lax
from jax.sharding import PartitionSpec as P

D = 3584
BLOCK = 128


def from_partner(block, axis, bit):
    count = lax.axis_size(axis)
    route = []
    for low in range(count):
        high = low | 1 << bit
        if high != low and high < count:
            route += [(low, high), (high, low)]
    return lax.ppermute(block, axis, route)


def encode(updated, codes, scale, mask):
    row_blocks, col_blocks = scale.shape
    base_vals = (
        codes.astype(jnp.float32).reshape(row_blocks, BLOCK, col_blocks, BLOCK)
        * scale[:, None, :, None]
    )
    change = updated.astype(jnp.float32).reshape(row_blocks, BLOCK, col_blocks, BLOCK) - base_vals
    peak_abs = jnp.max(jnp.abs(change), axis=(1, 3)) + 1e-06
    carries = mask[:, None, :, None] > 0
    scaled = jnp.where(carries, change / peak_abs[:, None, :, None], 0.0).astype(jnp.bfloat16)
    scaled = scaled.reshape(row_blocks * BLOCK, col_blocks * BLOCK)
    block_scales = jnp.where(mask > 0, peak_abs, 0.0).astype(jnp.bfloat16)
    return (scaled, block_scales)


def in_order(first_here, own_part, other_part):
    upper = jnp.where(first_here, own_part, other_part)
    lower = jnp.where(first_here, other_part, own_part)
    return jnp.concatenate([upper, lower], axis=0)


def body(new_weights, owner_map, block_mask, base_codes, base_scale):
    experts = owner_map.shape[0]
    owners = jnp.arange(experts, dtype=jnp.int32)
    holder = jnp.sum(jnp.where(owner_map[:, None] == owners[None, :], owners[:, None], 0), axis=0)
    ordered = jnp.take(new_weights, holder, axis=0)
    owner_slot = lax.axis_index("dev")
    section = lax.axis_index("group")
    half_rows = D // 2
    row_blocks = half_rows // BLOCK
    expert = holder[owner_slot]
    mask_rows = lax.dynamic_index_in_dim(block_mask, expert, 0, keepdims=False)
    mask_half = lax.dynamic_slice_in_dim(mask_rows, section * row_blocks, row_blocks, 0)
    arrived_rows = lax.all_to_all(ordered, "dev", split_axis=0, concat_axis=1, tiled=True)[0]
    code_half = lax.dynamic_slice_in_dim(base_codes[0], section * half_rows, half_rows, 0)
    scale_half = lax.dynamic_slice_in_dim(base_scale[0], section * row_blocks, row_blocks, 0)
    scaled, block_scales = encode(arrived_rows, code_half, scale_half, mask_half)
    other_rows, other_scales = from_partner((scaled, block_scales), "group", 0)
    first_here = section == 0
    full_delta = in_order(first_here, scaled, other_rows)
    full_scales = in_order(first_here, block_scales, other_scales)
    return (
        full_delta.reshape((1, 1) + full_delta.shape),
        full_scales.reshape((1, 1) + full_scales.shape),
    )


def solution(mesh):
    return jax.shard_map(
        body,
        mesh=mesh,
        in_specs=(
            P(None, ("group", "dev"), None),
            P(),
            P(),
            P("dev", None, None),
            P("dev", None, None),
        ),
        out_specs=(P("group", "dev", None, None), P("group", "dev", None, None)),
        check_vma=False,
    )
```

profile of v0, /device:TPU:0, one launch (start us, length us, event | category | flops | bytes accessed | tf_op | source)
XLA Modules:
  0.0 210.1 jit_solution(15855077151525082236)
XLA Ops:
  0.6 0.0 copy-start
  0.6 0.8 select_reduce_fusion
  1.5 11.2 %gather_fusion = bf16[64,28,1024]{2,0,1:T(8,128)(2,1)} fusion(bf16[64,28,1024]{2,0,1:T(8,128)(2,1)} %param.5, s32[1024]{0:T(1024)S(1)} %pad_clamp_fusion), kind=kCustom, calls=%fused_computation | custom fusion | bytes 7340288 | tf_op jit(solution)/shard_map/jit(_take)/gather | solution.py:45
  12.6 2.5 %broadcast_select_fusion = bf16[64,28,1024]{2,0,1:T(8,128)(2,1)S(1)} fusion(bf16[64,28,1024]{2,0,1:T(8,128)(2,1)} %gather_fusion, pred[64]{0:T(512)(128)(4,1)S(1)} %compare_and_fusion), kind=kLoop, calls=%fused_computation.13 | loop fusion | flops 1835008 | bytes 7340096 | tf_op jit(solution)/shard_map/jit(_take)/select_n | solution.py:45
  15.1 0.0 copy-start.2
  15.1 4.1 %copy.33 = bf16[64,28,1024]{2,1,0:T(8,128)(2,1)} copy(bf16[64,28,1024]{2,0,1:T(8,128)(2,1)S(1)} %broadcast_select_fusion) | data formatting | bytes 7340032 | tf_op jit(solution)/shard_map/jit(_take)/select_n | solution.py:45
  19.2 9.8 %all-to-all-start = ((bf16[64,28,1024]{2,1,0:T(8,128)(2,1)}), bf16[64,28,1024]{2,1,0:T(8,128)(2,1)}, u32[]{:S(2)}, u32[]{:S(2)}) async-start(bf16[64,28,1024]{2,1,0:T(8,128)(2,1)} %copy.33), calls=%async_computation | async-start | bytes 8388608 | tf_op jit(solution)/shard_map/all_to_all | solution.py:53
  29.0 0.6 dynamic_slice.14
  31.6 0.0 copy-done
  31.6 0.1 constant_dynamic-slice_fusion
  31.6 0.1 copy.38
  31.8 0.1 copy.32
  31.9 0.0 copy-done.2
  31.9 0.1 dynamic-slice_bitcast_fusion
  32.0 0.1 copy.34
  32.1 2.9 %convert_bitcast_fusion = f32[224,8,8,128]{3,1,2,0:T(8,128)S(1)} fusion(bf16[1,3584,1024]{2,1,0:T(8,128)(2,1)} %param.8, s32[]{:T(128)S(6)} %select_n.85), kind=kLoop, calls=%fused_computation.1 | loop fusion | flops 1835008 | bytes 11010052
  35.0 4.8 %copy.41 = f32[224,8,8,128]{3,2,1,0:T(8,128)} copy(f32[224,8,8,128]{3,1,2,0:T(8,128)S(1)} %convert_bitcast_fusion) | data formatting | bytes 14680064
  39.7 41.7 %all-to-all-done = bf16[64,28,1024]{2,1,0:T(8,128)(2,1)} async-done(((bf16[64,28,1024]{2,1,0:T(8,128)(2,1)}), bf16[64,28,1024]{2,1,0:T(8,128)(2,1)}, u32[]{:S(2)}, u32[]{:S(2)}) %all-to-all-start) | async-done | bytes 3670048 | tf_op jit(solution)/shard_map/all_to_all | solution.py:53
  81.5 7.7 %reshape.74 = f32[14,128,8,128]{3,2,1,0:T(8,128)} reshape(bf16[64,28,1024]{2,1,0:T(8,128)(2,1)} %all-to-all-done) | data formatting | bytes 11010048 | tf_op jit(solution)/shard_map/convert_element_type | solution.py:26
  89.1 6.2 %fusion.6 = f32[14,8]{1,0:T(8,128)S(1)} fusion(f32[14,128,8,128]{3,2,1,0:T(8,128)} %reshape.74, f32[14,8]{1,0:T(8,128)S(1)} %copy.34, f32[14,128,8,128]{3,2,1,0:T(8,128)} %bitcast.54), kind=kLoop, calls=%fused_computation.10 | loop fusion | flops 7339920 | bytes 14680960 | tf_op jit(solution)/shard_map/reduce_max | solution.py:27
  95.4 6.7 %reshape.72 = f32[1792,1024]{1,0:T(8,128)} reshape(bf16[64,28,1024]{2,1,0:T(8,128)(2,1)} %all-to-all-done) | data formatting | bytes 11010048 | tf_op jit(solution)/shard_map/convert_element_type | solution.py:26
  102.1 0.0 slice-start
  102.1 0.5 div.11
  102.7 0.0 slice-start.1
  102.7 0.5 mul.25
  103.2 1.8 broadcast_in_dim.48
  105.0 0.0 slice-done
  105.0 1.1 slice-done.1
  106.1 9.0 %fusion.7 = bf16[1792,1024]{1,0:T(8,128)(2,1)} fusion(f32[224,8,8,128]{3,2,1,0:T(8,128)S(1)} %bitcast.57, f32[1792,1024]{1,0:T(8,128)S(1)} %bitcast.56, f32[224,8,8,128]{3,2,1,0:T(8,128)S(1)} %bitcast.58, pred[224,8,8,128]{3,2,1,0:T(8,128)(4,1)} %bitcast.59, bf16[1,3584,1024]{2,1,0:T(8,128)(2,1)} %param.8, s32[]{:T(128)S(6)} %select_n.85), kind=kLoop, calls=%fused_computation.12 | loop fusion | flops 11010048 | bytes 31195140 | tf_op jit(solution)/shard_map/convert_element_type | solution.py:29
  115.1 3.6 %collective-permute-start = (bf16[1792,1024]{1,0:T(8,128)(2,1)}, bf16[1792,1024]{1,0:T(8,128)(2,1)}, u32[]{:S(2)}, u32[]{:S(2)}) collective-permute-start(bf16[1792,1024]{1,0:T(8,128)(2,1)} %fusion.7), channel_id=1, source_target_pairs={{0,64},{64,0},{1,65},{65,1},{2,66},{66,2},{3,67},{67,3},{4,68},{68... | collective-permute-start | bytes 11010056 | tf_op jit(solution)/shard_map/ppermute | solution.py:17
  118.7 0.0 collective-permute-start.1
  118.7 79.1 %collective-permute-done.1 = bf16[14,8]{1,0:T(8,128)(2,1)S(1)} collective-permute-done((bf16[14,8]{1,0:T(8,128)(2,1)S(1)}, bf16[14,8]{1,0:T(8,128)(2,1)S(1)}, u32[]{:S(2)}, u32[]{:S(2)}) %collective-permute-start.1) | collective-permute-done | bytes 256 | tf_op jit(solution)/shard_map/ppermute | solution.py:17
  197.8 0.1 copy.37
  197.9 0.1 copy.36
  198.0 0.7 maximum_bitcast_fusion.1
  198.7 0.0 collective-permute-done
  198.7 5.5 %broadcast_select_fusion.2 = (bf16[1792,1024]{1,0:T(8,128)(2,1)S(1)}, bf16[1792,1024]{1,0:T(8,128)(2,1)}) fusion(bf16[1792,1024]{1,0:T(8,128)(2,1)} %fusion.7, bf16[1792,1024]{1,0:T(8,128)(2,1)} %collective-permute-done, pred[]{:T(512)S(6)} %eq.16), kind=kLoop, calls=%fused_computation.15 | loop fusion | flops 3670016 | bytes 14680065 | tf_op jit(solution)/shard_map/jit(_where)/select_n | solution.py:36
  204.1 0.0 copy-start.1
  204.1 6.0 %maximum_bitcast_fusion = bf16[1,1,3584,1024]{3,2,1,0:T(8,128)(2,1)} fusion(bf16[1792,1024]{1,0:T(8,128)(2,1)} %get-tuple-element.5, bf16[1792,1024]{1,0:T(8,128)(2,1)S(1)} %get-tuple-element.4), kind=kLoop, calls=%fused_computation.11 | loop fusion | flops 14680064 | bytes 14680064 | tf_op jit(solution)/shard_map/reshape | solution.py:62
  210.1 0.0 copy-done.1
  (7 shorter events, 0.0 us)
Async XLA Ops:
  0.6 30.9 %copy-start = (s32[64,28,8]{0,2,1:T(8,128)S(1)}, s32[64,28,8]{0,2,1:T(8,128)}, u32[]{:S(2)}) copy-start(s32[64,28,8]{0,2,1:T(8,128)} %param.7) | copy-start | bytes 172036
  15.1 16.8 %copy-start.2 = (f32[1,28,8]{1,2,0:T(8,128)S(1)}, f32[1,28,8]{1,2,0:T(8,128)}, u32[]{:S(2)}) copy-start(f32[1,28,8]{1,2,0:T(8,128)} %param.9) | copy-start | bytes 2692
  19.2 62.3 %all-to-all-start = ((bf16[64,28,1024]{2,1,0:T(8,128)(2,1)}), bf16[64,28,1024]{2,1,0:T(8,128)(2,1)}, u32[]{:S(2)}, u32[]{:S(2)}) async-start(bf16[64,28,1024]{2,1,0:T(8,128)(2,1)} %copy.33), calls=%async_computation | async-start | bytes 8388608 | tf_op jit(solution)/shard_map/all_to_all | solution.py:53
  102.1 2.9 %slice-start = ((s8[7340032]{0:T(1024)(128)(4,1)}), s8[4194304]{0:T(1024)(128)(4,1)S(1)}, s32[]{:S(2)}) async-start(s8[7340032]{0:T(1024)(128)(4,1)} %bitcast.55), calls=%async_computation.1 | async-start | bytes 8388608
  102.7 3.4 %slice-start.1 = ((s8[7340032]{0:T(1024)(128)(4,1)}), s8[3145728]{0:T(1024)(128)(4,1)S(1)}, s32[]{:S(2)}) async-start(s8[7340032]{0:T(1024)(128)(4,1)} %bitcast.55), calls=%async_computation.2 | async-start | bytes 6291456
  115.1 83.6 %collective-permute-start = (bf16[1792,1024]{1,0:T(8,128)(2,1)}, bf16[1792,1024]{1,0:T(8,128)(2,1)}, u32[]{:S(2)}, u32[]{:S(2)}) collective-permute-start(bf16[1792,1024]{1,0:T(8,128)(2,1)} %fusion.7), channel_id=1, source_target_pairs={{0,64},{64,0},{1,65},{65,1},{2,66},{66,2},{3,67},{67,3},{4,68},{68... | collective-permute-start | bytes 11010056 | tf_op jit(solution)/shard_map/ppermute | solution.py:17
  118.7 79.1 %collective-permute-start.1 = (bf16[14,8]{1,0:T(8,128)(2,1)S(1)}, bf16[14,8]{1,0:T(8,128)(2,1)S(1)}, u32[]{:S(2)}, u32[]{:S(2)}) collective-permute-start(bf16[14,8]{1,0:T(8,128)(2,1)S(1)} %get-tuple-element.8), channel_id=1, source_target_pairs={{0,64},{64,0},{1,65},{65,1},{2,66},{66,2},{3,67},{67,3},{4,68},{68... | collective-permute-start | bytes 680 | tf_op jit(solution)/shard_map/ppermute | solution.py:17
  204.1 6.0 %copy-start.1 = (s32[64,28,8]{0,2,1:T(8,128)S(1)}, s32[64,28,8]{0,2,1:T(8,128)}, u32[]{:S(2)}) copy-start(s32[64,28,8]{0,2,1:T(8,128)} %param.7) | copy-start | bytes 172036
where the time goes:
time: 211 us; the launch traced here: 210 us
  waiting for transfers between devices  121 us (57%)
  local copies, waits for them, and re-layouts  39.6 us (19%)
  other arithmetic  33.5 us (16%)
  starting transfers between devices  13.4 us (6%)
  between operations  2.7 us (1%)
    ppermute x2, waiting for transfers between devices, from_partner(): return lax.ppermute(block, axis, route)  79.1 us
    all_to_all x1, waiting for transfers between devices, body(): lax.all_to_all(ordered, 'dev', split_axis=0, concat_axis=1, tiled=True)[0]  41.7 us
    convert_element_type x2, local copies, waits for them, and re-layouts, encode(): updated.astype(jnp.float32).reshape(row_blocks, BLOCK, col_blocks, BLOCK)  14.4 us
    gather x1, local copies, waits for them, and re-layouts, body(): ordered = jnp.take(new_weights, holder, axis=0)  11.2 us
    all_to_all x1, starting transfers between devices, body(): lax.all_to_all(ordered, 'dev', split_axis=0, concat_axis=1, tiled=True)[0]  9.82 us
    convert_element_type x1, other arithmetic, encode(): jnp.where(carries, change / peak_abs[:, None, :, None], 0.0)  9.02 us
    reduce_max x1, other arithmetic, encode(): peak_abs = jnp.max(jnp.abs(change), axis=(1, 3)) + 1e-06  6.24 us
    unnamed x12, local copies, waits for them, and re-layouts  6 us
  transfers between devices with their start and end apart: 3, of which 2 were waited for; matrix products, arithmetic and copies ran while one was open for 5% of the time, Pallas kernels for 0%

commit v1 on v0

v1 whole, which is shorter than its diff:
```python
import jax
import jax.numpy as jnp
from jax import lax
from jax.experimental import pallas as pl
from jax.experimental.pallas import tpu as pltpu
from jax.sharding import PartitionSpec as P

BLOCK = 128
MESH = pl.DeviceIdType.MESH
OWNERS = 64
GROUPS = 2
SHARD = 28
ROW_BLOCKS = 28
COL_BLOCKS = 8
CARRIED = 4
MAIN = 24
PIECE = SHARD * CARRIED


def owner_at(me, t):
    core, y, zl, x = me % 2, (me // 2) % 4, (me // 8) % 2, me // 16
    a, b, e = t % 4, (t // 4) % 4, t // 16
    v = (a + b + e) % 4
    x = (x + a) % 4
    y = (y + a + b) % 4
    zl = (zl + v) % 2
    core = (core + v // 2) % 2
    return ((x * 2 + zl) * 4 + y) * 2 + core


def exchange(holder, places, weights, recv, mine, send, load_sem, own_sem, send_sem, recv_sem):
    g = lax.axis_index("group")
    me = lax.axis_index("dev")
    my_id = g * OWNERS + me

    barrier = pltpu.get_barrier_semaphore()

    def greet(i, carry):
        other = (my_id + i) % (GROUPS * OWNERS)
        pl.semaphore_signal(
            barrier, inc=1, device_id=(other // OWNERS, other % OWNERS), device_id_type=MESH
        )
        return carry

    loads = [
        pltpu.make_async_copy(
            weights.at[:, :, pl.ds(BLOCK * c, BLOCK)], mine.at[c], load_sem.at[c]
        )
        for c in range(COL_BLOCKS)
    ]
    for load in loads:
        load.start()
    lax.fori_loop(1, GROUPS * OWNERS, greet, 0)
    for load in loads:
        load.wait()

    first_row = my_id * SHARD
    block_a = first_row // BLOCK
    block_b = jnp.minimum(block_a + 1, ROW_BLOCKS - 1)
    split = (block_a + 1) * BLOCK - first_row
    phase = me % 2
    row = lax.broadcasted_iota(jnp.int32, (SHARD, BLOCK), 0)
    in_a = row < split
    sub = lax.broadcasted_iota(jnp.int32, (8, BLOCK), 0)
    straight = (sub // 4) == phase

    def pack(t):
        e = holder[owner_at(me, t)]
        code_a = places[e, block_a]
        code_b = places[e, block_b]
        mains, rests = [], []
        for k in range(CARRIED):
            rows_a = mine[(code_a >> (3 * k)) & 7, e].astype(jnp.float32)
            rows_b = mine[(code_b >> (3 * k)) & 7, e].astype(jnp.float32)
            rows = jnp.where(in_a, rows_a, rows_b)
            rows = jnp.concatenate([rows, jnp.zeros((4, BLOCK), jnp.float32)], axis=0)
            rows = jnp.where(phase == 1, jnp.roll(rows, -4, axis=0), rows)
            mains.append(rows[:MAIN])
            rests.append(rows[MAIN:])
        left_a = jnp.where(straight, rests[0], jnp.roll(rests[1], 4, axis=0))
        left_b = jnp.where(straight, rests[2], jnp.roll(rests[3], 4, axis=0))
        send[t] = jnp.concatenate(mains + [left_a, left_b], axis=0).astype(jnp.bfloat16)

    def to(t, gt):
        return pltpu.make_async_remote_copy(
            src_ref=send.at[t],
            dst_ref=recv.at[my_id],
            send_sem=send_sem,
            recv_sem=recv_sem,
            device_id=(gt, owner_at(me, t)),
            device_id_type=MESH,
        )

    pack(0)
    keep = pltpu.make_async_copy(send.at[0], recv.at[my_id], own_sem)
    keep.start()
    pl.semaphore_wait(barrier, GROUPS * OWNERS - 1)
    to(0, 1 - g).start()

    def step(t, carry):
        pack(t)
        to(t, g).start()
        to(t, 1 - g).start()
        return carry

    lax.fori_loop(1, OWNERS, step, 0)

    keep.wait()
    sent = recv.at[pl.ds(0, GROUPS * OWNERS - 1)]
    pltpu.make_async_copy(sent, sent, send_sem).wait()
    pltpu.make_async_copy(sent, sent, recv_sem).wait()


def decode(places, scales, recv, codes, out, out_scales):
    group = pl.program_id(0)
    sub = lax.broadcasted_iota(jnp.int32, (8, BLOCK), 0)
    low = sub < 4
    lane = lax.broadcasted_iota(jnp.int32, (1, BLOCK), 1)
    per = ROW_BLOCKS // 4
    out[...] = jnp.zeros_like(out)

    def pair_rows(m, k):
        even = recv[2 * m].astype(jnp.float32)
        odd = recv[2 * m + 1].astype(jnp.float32)
        at = CARRIED * MAIN + 8 * (k // 2)
        rest_even, rest_odd = even[at : at + 8], odd[at : at + 8]
        if k % 2 == 0:
            middle = jnp.where(low, rest_even, rest_odd)
        else:
            middle = jnp.roll(jnp.where(low, rest_odd, rest_even), 4, axis=0)
        return [even[MAIN * k : MAIN * (k + 1)], middle, odd[MAIN * k : MAIN * (k + 1)]]

    for r in range(per):
        a = group * per + r
        code = places[a]
        scale_row = jnp.zeros((1, BLOCK), jnp.float32)
        for k in range(CARRIED):
            rows = []
            first, last = BLOCK * r, BLOCK * (r + 1)
            for m in range(first // 56, (last + 55) // 56):
                whole = jnp.concatenate(pair_rows(m, k), axis=0)
                rows.append(whole[max(first - 56 * m, 0) : min(last - 56 * m, 56)])
            updated = jnp.concatenate(rows, axis=0)
            col = (code >> (3 * k)) & 7
            at = pl.ds(pl.multiple_of(col * BLOCK, BLOCK), BLOCK)
            here = pl.ds(BLOCK * r, BLOCK)
            change = updated - codes[here, at].astype(jnp.float32) * scales[a, col]
            peak = jnp.max(jnp.max(jnp.abs(change), axis=0, keepdims=True), axis=1, keepdims=True) + 1e-06
            out[here, at] = (change * (1.0 / peak)).astype(jnp.bfloat16)
            scale_row = jnp.where(lane == col, peak, scale_row)
        out_scales[pl.ds(a, 1), :] = scale_row[:, :COL_BLOCKS]


def body(new_weights, owner_map, block_mask, base_codes, base_scale):
    owners = jnp.arange(OWNERS, dtype=jnp.int32)
    holder = jnp.sum(jnp.where(owner_map[:, None] == owners[None, :], owners[:, None], 0), axis=0)
    carried = block_mask > 0
    upto = jnp.zeros(carried.shape[:2], jnp.int32)
    places = jnp.zeros(carried.shape[:2], jnp.int32)
    for c in range(COL_BLOCKS):
        here = carried[:, :, c]
        places = places + jnp.where(here, c << upto, 0)
        upto = upto + jnp.where(here, 3, 0)

    recv = pl.pallas_call(
        exchange,
        out_shape=jax.ShapeDtypeStruct((GROUPS * OWNERS, PIECE, BLOCK), jnp.bfloat16),
        in_specs=[
            pl.BlockSpec(memory_space=pltpu.SMEM),
            pl.BlockSpec(memory_space=pltpu.SMEM),
            pl.BlockSpec(memory_space=pl.ANY),
        ],
        out_specs=pl.BlockSpec(memory_space=pl.ANY),
        scratch_shapes=[
            pltpu.VMEM((COL_BLOCKS, OWNERS, SHARD, BLOCK), jnp.bfloat16),
            pltpu.VMEM((OWNERS, PIECE, BLOCK), jnp.bfloat16),
            pltpu.SemaphoreType.DMA((COL_BLOCKS,)),
            pltpu.SemaphoreType.DMA,
            pltpu.SemaphoreType.DMA,
            pltpu.SemaphoreType.DMA,
        ],
        compiler_params=pltpu.CompilerParams(
            collective_id=0, has_side_effects=True, vmem_limit_bytes=32 * 2**20
        ),
        name="exchange",
    )(holder, places, new_weights)

    own = places[holder[lax.axis_index("dev")]]
    per = ROW_BLOCKS // 4
    deltas, scales = pl.pallas_call(
        decode,
        grid=(4,),
        out_shape=(
            jax.ShapeDtypeStruct(base_codes.shape[1:], jnp.bfloat16),
            jax.ShapeDtypeStruct((ROW_BLOCKS, COL_BLOCKS), jnp.float32),
        ),
        in_specs=[
            pl.BlockSpec(memory_space=pltpu.SMEM),
            pl.BlockSpec(memory_space=pltpu.SMEM),
            pl.BlockSpec((32, PIECE, BLOCK), lambda i: (i, 0, 0)),
            pl.BlockSpec((per * BLOCK, COL_BLOCKS * BLOCK), lambda i: (i, 0)),
        ],
        out_specs=(
            pl.BlockSpec((per * BLOCK, COL_BLOCKS * BLOCK), lambda i: (i, 0)),
            pl.BlockSpec((ROW_BLOCKS, COL_BLOCKS), lambda i: (0, 0)),
        ),
        compiler_params=pltpu.CompilerParams(vmem_limit_bytes=48 * 2**20),
        name="decode",
    )(own, base_scale[0], recv, base_codes[0])
    return deltas[None, None], scales.astype(jnp.bfloat16)[None, None]


def solution(mesh):
    return jax.shard_map(
        body,
        mesh=mesh,
        in_specs=(
            P(None, ("group", "dev"), None),
            P(),
            P(),
            P("dev", None, None),
            P("dev", None, None),
        ),
        out_specs=(P("group", "dev", None, None), P("group", "dev", None, None)),
        check_vma=False,
    )
```

time: 211 us -> 77.4 us (0.37)
  waiting for transfers between devices: 121 us -> 0 us
  Pallas kernels: 0 us -> 66.2 us
  other arithmetic: 33.5 us -> 0.85 us
  local copies, waits for them, and re-layouts: 39.6 us -> 7.16 us
  starting transfers between devices: 13.4 us -> 0 us
    ppermute x2 -> x0, waiting for transfers between devices: 79.1 us -> none  [from_partner(): return lax.ppermute(block, axis, route)]
    pallas_call x0 -> x2, Pallas kernels: none -> 66.2 us  [the longest x1 58.6 us: body(): pl.pallas_call(exchange, out_shape=jax.ShapeDtypeStruct((GROUPS * OWNERS,...]
    all_to_all x1 -> x0, waiting for transfers between devices: 41.7 us -> none  [body(): lax.all_to_all(ordered, 'dev', split_axis=0, concat_axis=1, tiled=True)[0]]
    convert_element_type x2 -> x0, local copies, waits for them, and re-layouts: 14.4 us -> none  [encode(): updated.astype(jnp.float32).reshape(row_blocks, BLOCK, col_blocks, BLOCK)]
    gather x1 -> x0, local copies, waits for them, and re-layouts: 11.2 us -> none  [body(): ordered = jnp.take(new_weights, holder, axis=0)]
    all_to_all x1 -> x0, starting transfers between devices: 9.82 us -> none  [body(): lax.all_to_all(ordered, 'dev', split_axis=0, concat_axis=1, tiled=True)[0]]
    convert_element_type x2 -> x0, other arithmetic: 9.03 us -> none  [the longest x1 9.02 us: encode(): jnp.where(carries, change / peak_abs[:, None, :, None], 0.0)]
    select_n x4 -> x0, other arithmetic: 7.92 us -> none  [the longest x2 5.46 us: in_order(): upper = jnp.where(first_here, own_part, other_part)]
  transfers between devices with their start and end apart: 3 -> 0, of which waited for: 2 -> 0; matrix products, arithmetic and copies ran while one was open for 5% -> 0% of each run, Pallas kernels for 0% -> 0%
where the time goes in v1:
time: 77.4 us; the launch traced here: 76.9 us
  Pallas kernels  66.2 us (86%)
  local copies, waits for them, and re-layouts  7.16 us (9%)
  between operations  2.63 us (3%)
  other arithmetic  0.85 us (1%)
    pallas_call x1, Pallas kernels, body(): pl.pallas_call(exchange, out_shape=jax.ShapeDtypeStruct((GROUPS * OWNERS,...  58.6 us
    pallas_call x1, Pallas kernels, body(): pl.pallas_call(decode, grid=(4,), out_shape=(jax.ShapeDtypeStruct(base_co...  7.68 us
    unnamed x4, local copies, waits for them, and re-layouts  6.56 us

profile of v1, /device:TPU:0, one launch (start us, length us, event | category | flops | bytes accessed | tf_op | source)
XLA Modules:
  0.0 76.9 jit_solution(9857470080487848211)
XLA Ops:
  0.6 0.7 select_reduce_fusion.holder
  1.4 0.6 dynamic_slice.6
  3.9 0.8 %copy.12 = f32[1,28,8]{2,1,0:T(8,128)S(1)} copy(f32[1,28,8]{1,2,0:T(8,128)} %param.9) | data formatting | bytes 1792 | tf_op args[4]
  4.7 1.0 %copy.11 = s32[64,28,8]{1,0,2:T(8,128)S(1)} copy(s32[64,28,8]{0,2,1:T(8,128)} %param.7) | data formatting | bytes 114688 | tf_op args[2]
  5.8 0.1 fusion.6.places
  5.9 4.1 %copy.13.weights = bf16[64,28,1024]{2,1,0:T(8,128)(2,1)S(1)} copy(bf16[64,28,1024]{2,0,1:T(8,128)(2,1)} %param.5) | data formatting | bytes 7340032 | tf_op args[0]
  10.0 58.6 %exchange.1.recv = bf16[128,112,128]{2,1,0:T(8,128)(2,1)S(1)} custom-call(s32[64]{0:T(128)S(1)} %select_reduce_fusion.holder, s32[64,28]{1,0:T(8,128)S(1)} %fusion.6.places, bf16[64,28,1024]{2,1,0:T(8,128)(2,1)S(1)} %copy.13.weights), custom_call_target="tpu_custom_call" | custom-call | tf_op jit(solution)/shard_map/exchange/pallas_call | solution.py:165
  68.5 7.7 %decode.1 = (bf16[3584,1024]{1,0:T(8,128)(2,1)}, f32[28,8]{1,0:T(8,128)S(1)}) custom-call(s32[28]{0:T(128)S(1)} %dynamic-slice_bitcast_fusion.places, f32[28,8]{1,0:T(8,128)S(1)} %bitcast.55, bf16[128,112,128]{2,1,0:T(8,128)(2,1)S(1)} %exchange.1.recv, bf16[3584,1024]{1,0:T(8,128)(2,1)} %bitcast.56), custom_call_target="tpu_custom_call" | custom-call | tf_op jit(solution)/shard_map/decode/pallas_call | solution.py:190
  76.2 0.7 copy.14
  (3 shorter events, 0.1 us)

commit v2 on v1

v2 whole, which is shorter than its diff:
```python
import jax
import jax.numpy as jnp
from jax import lax
from jax.experimental import pallas as pl
from jax.experimental.pallas import tpu as pltpu
from jax.sharding import PartitionSpec as P

BLOCK = 128
MESH = pl.DeviceIdType.MESH
OWNERS = 64
GROUPS = 2
PEERS = GROUPS * OWNERS - 1
SHARD = 28
ROW_BLOCKS = 28
COL_BLOCKS = 8
CARRIED = 4
MAIN = 24
PIECE = SHARD * CARRIED
PAIR = 2 * SHARD
SETS = 4
PER_SET = ROW_BLOCKS // SETS
CHUNKS = 7
CHUNK = 4 * OWNERS
HALF = OWNERS // 2


def owner_at(me, t):
    core, y, zl, x = me % 2, (me // 2) % 4, (me // 8) % 2, me // 16
    a, b, e = t % 4, (t // 4) % 4, t // 16
    v = (a + b + e) % 4
    x = (x + a) % 4
    y = (y + a + b) % 4
    zl = (zl + v) % 2
    core = (core + v // 2) % 2
    return ((x * 2 + zl) * 4 + y) * 2 + core


def places_of(mask):
    axis = mask.ndim - 2
    column = lax.broadcasted_iota(jnp.int32, mask.shape, axis)
    upto = mask
    for step in (1, 2, 4):
        upto = upto + jnp.where(column >= step, pltpu.roll(upto, step, axis), 0)
    value = jnp.zeros_like(mask)
    for k in range(CARRIED):
        value = value + jnp.where(upto == k + 1, column << (3 * k), 0)
    return jnp.sum(jnp.where(mask > 0, value, 0), axis=axis, keepdims=True)


def column_of(code, k):
    return (code >> (3 * k)) & 7


def exchange(
    owner_map, mask, scales, codes, weights, recv, own, scales_out, codes_out,
    owners, masks, tile, table, raw, by_expert, turn, turn_rest, send,
    small_sems, load_sems, keep_sem, send_sem, recv_sem,
):
    g = lax.axis_index("group")
    me = lax.axis_index("dev")
    my_id = g * OWNERS + me
    first_row = my_id * SHARD
    block_a = first_row // BLOCK
    block_b = jnp.minimum(block_a + 1, ROW_BLOCKS - 1)
    split = (block_a + 1) * BLOCK - first_row
    phase = me % 2

    barrier = pltpu.get_barrier_semaphore()

    def greet(i, carry):
        other = (my_id + i) % (GROUPS * OWNERS)
        pl.semaphore_signal(
            barrier, inc=1, device_id=(other // OWNERS, other % OWNERS), device_id_type=MESH
        )
        return carry

    def load(i):
        rows = pl.ds(pl.multiple_of(i * CHUNK, CHUNK), CHUNK)
        return pltpu.make_async_copy(weights.at[rows], raw.at[rows], load_sems.at[i])

    load_owners = pltpu.make_async_copy(owner_map, owners, small_sems.at[0])
    load_masks = pltpu.make_async_copy(mask, masks, small_sems.at[1])
    load_scales = pltpu.make_async_copy(scales, scales_out, small_sems.at[2])
    load_codes = pltpu.make_async_copy(codes, codes_out, small_sems.at[4])
    load_owners.start()
    load_masks.start()
    for i in range(CHUNKS):
        load(i).start()
    lax.fori_loop(1, GROUPS * OWNERS, greet, 0)
    load_scales.start()
    load_codes.start()

    to_row = lax.broadcasted_iota(jnp.int32, (256, 256), 0)
    from_row = lax.broadcasted_iota(jnp.int32, (256, 256), 1)
    same = (to_row // 8 == from_row % HALF) & (to_row % 8 == from_row // HALF)
    turn[...] = jnp.where(same, 1.0, 0.0).astype(jnp.bfloat16)
    same = (to_row // 8 == from_row % HALF) & (to_row % 8 == from_row // HALF + 4 * phase)
    turn_rest[...] = jnp.where(same, 1.0, 0.0).astype(jnp.bfloat16)[:, :BLOCK]

    load_owners.wait()
    sub = lax.broadcasted_iota(jnp.int32, (OWNERS, OWNERS), 0)
    lane = lax.broadcasted_iota(jnp.int32, (OWNERS, OWNERS), 1)
    owner_row = owners[...]
    owner_column = jnp.sum(jnp.where(sub == lane, owner_row, 0), axis=1, keepdims=True)
    holder = jnp.sum(jnp.where(owner_column == lane, sub, 0), axis=0, keepdims=True)
    tile[2:3, :OWNERS] = jnp.minimum(holder, OWNERS - 1)
    load_masks.wait()
    tile[0:1, :OWNERS] = places_of(masks[block_a])
    tile[1:2, :OWNERS] = places_of(masks[block_b])
    to_table = pltpu.make_async_copy(tile, table, small_sems.at[3])
    to_table.start()

    def regroup(first, count, matrix, at):
        for h in range(2):
            for c in range(COL_BLOCKS // 2):
                cols = pl.ds(2 * BLOCK * c, 2 * BLOCK)
                part = [
                    raw[pl.ds(pl.multiple_of((first + r) * OWNERS + h * HALF, HALF), HALF), cols]
                    for r in range(count)
                ]
                found = jnp.dot(
                    matrix[...], jnp.concatenate(part, axis=0), preferred_element_type=jnp.float32
                )
                for u in range(2):
                    by_expert[2 * c + u, HALF * h : HALF * (h + 1), at : at + 8, :] = found[
                        :, BLOCK * u : BLOCK * (u + 1)
                    ].reshape(HALF, 8, BLOCK)

    for i in range(3):
        load(phase + 2 * i).wait()
        load(phase + 2 * i + 1).wait()
        regroup(4 * phase + 8 * i, 8, turn, 8 * i)
    load(6 - 6 * phase).wait()
    regroup(24 - 24 * phase, 4, turn_rest, MAIN)
    to_table.wait()

    row = lax.broadcasted_iota(jnp.int32, (MAIN + 8, BLOCK), 0)
    row = row + jnp.where(row < MAIN, 4 * phase, -28 * phase)
    in_a = row < split
    straight = (lax.broadcasted_iota(jnp.int32, (8, BLOCK), 0) // 4) == phase

    def pack(t):
        e = table[2, owner_at(me, t)]
        code_a, code_b = table[0, e], table[1, e]
        mains, rests = [], []
        for k in range(CARRIED):
            rows = jnp.where(in_a, by_expert[column_of(code_a, k), e], by_expert[column_of(code_b, k), e])
            mains.append(rows[:MAIN])
            rests.append(rows[MAIN:])
        left_a = jnp.where(straight, rests[0], pltpu.roll(rests[1], 4, 0))
        left_b = jnp.where(straight, rests[2], pltpu.roll(rests[3], 4, 0))
        send[t] = jnp.concatenate(mains + [left_a, left_b], axis=0).astype(jnp.bfloat16)

    def to(t, gt):
        return pltpu.make_async_remote_copy(
            src_ref=send.at[t],
            dst_ref=recv.at[my_id],
            send_sem=send_sem,
            recv_sem=recv_sem,
            device_id=(gt, owner_at(me, t)),
            device_id_type=MESH,
        )

    pack(0)
    keep = pltpu.make_async_copy(send.at[0], recv.at[my_id], keep_sem)
    keep.start()
    pl.semaphore_wait(barrier, PEERS)
    to(0, 1 - g).start()

    def step(t, carry):
        pack(t)
        to(t, g).start()
        to(t, 1 - g).start()
        return carry

    lax.fori_loop(1, OWNERS, step, 0)

    mine = jnp.sum(jnp.where(owner_row[None] == me, masks[...], 0), axis=2, keepdims=True)
    mine = places_of(jnp.broadcast_to(mine, (ROW_BLOCKS, COL_BLOCKS, BLOCK)))
    lane = lax.broadcasted_iota(jnp.int32, mine.shape, 2)
    block = lax.broadcasted_iota(jnp.int32, mine.shape, 0)
    own[...] = jnp.sum(jnp.where(lane == block, mine, 0), axis=0)

    load_scales.wait()
    load_codes.wait()
    keep.wait()
    sent = recv.at[pl.ds(0, PEERS)]
    pltpu.make_async_copy(sent, sent, send_sem).wait()
    pltpu.make_async_copy(sent, sent, recv_sem).wait()


def decode(own, scales, held, base, out, out_scales, change, peaks, made, out_sem):
    low = lax.broadcasted_iota(jnp.int32, (8, BLOCK), 0) < 4
    lane = lax.broadcasted_iota(jnp.int32, (COL_BLOCKS, BLOCK), 1)
    column = lax.broadcasted_iota(jnp.int32, (COL_BLOCKS, BLOCK), 0)
    per_set = GROUPS * OWNERS // SETS
    pairs = per_set // 2

    def one_set(s, found):
        rows_of = [[[] for k in range(CARRIED)] for r in range(PER_SET)]
        for r in range(PER_SET):
            a = s * PER_SET + r
            here = pl.ds(pl.multiple_of(a * BLOCK, BLOCK), BLOCK)
            made[here, :] = jnp.zeros((BLOCK, COL_BLOCKS * BLOCK), jnp.bfloat16)
        for r in range(PER_SET):
            a = s * PER_SET + r
            here = pl.ds(pl.multiple_of(a * BLOCK, BLOCK), BLOCK)
            code = own[0, a]
            first, last = BLOCK * r, BLOCK * (r + 1)
            parts = [[] for k in range(CARRIED)]
            for m in range(first // PAIR, (last + PAIR - 1) // PAIR):
                even = held[s * per_set + 2 * m].astype(jnp.float32)
                odd = held[s * per_set + 2 * m + 1].astype(jnp.float32)
                for k in range(CARRIED):
                    at = CARRIED * MAIN + 8 * (k // 2)
                    rest_even, rest_odd = even[at : at + 8], odd[at : at + 8]
                    if k % 2 == 0:
                        middle = jnp.where(low, rest_even, rest_odd)
                    else:
                        middle = pltpu.roll(jnp.where(low, rest_odd, rest_even), 4, 0)
                    whole = jnp.concatenate(
                        [even[MAIN * k : MAIN * (k + 1)], middle, odd[MAIN * k : MAIN * (k + 1)]], axis=0
                    )
                    parts[k].append(whole[max(first - PAIR * m, 0) : min(last - PAIR * m, PAIR)])
            for k in range(CARRIED):
                col = column_of(code, k)
                at = pl.ds(pl.multiple_of(col * BLOCK, BLOCK), BLOCK)
                diff = jnp.concatenate(parts[k], axis=0) - base[here, at].astype(jnp.float32) * scales[col, a]
                change[r * CARRIED + k] = diff
                peaks[r * CARRIED + k] = jnp.max(jnp.abs(diff).reshape(16, 8, BLOCK), axis=0)
        peak = jnp.max(jnp.max(peaks[...], axis=1, keepdims=True), axis=2, keepdims=True) + 1e-06
        inverse = 1.0 / peak
        for r in range(PER_SET):
            a = s * PER_SET + r
            here = pl.ds(pl.multiple_of(a * BLOCK, BLOCK), BLOCK)
            code = own[0, a]
            for k in range(CARRIED):
                i = r * CARRIED + k
                col = column_of(code, k)
                at = pl.ds(pl.multiple_of(col * BLOCK, BLOCK), BLOCK)
                made[here, at] = (change[i] * inverse[i]).astype(jnp.bfloat16)
                found = jnp.where((lane == a) & (column == col), peak[i], found)
            pltpu.make_async_copy(made.at[here], out.at[here], out_sem).start()
        return found

    found = lax.fori_loop(0, SETS, one_set, jnp.zeros((COL_BLOCKS, BLOCK), jnp.float32))
    out_scales[...] = found[:, :ROW_BLOCKS].astype(jnp.bfloat16)
    pltpu.make_async_copy(made, out, out_sem).wait()


def body(new_weights, owner_map, block_mask, base_codes, base_scale):
    weights = new_weights.transpose(1, 0, 2).reshape(SHARD * OWNERS, COL_BLOCKS * BLOCK)
    mask = block_mask.transpose(1, 2, 0)
    smem = pl.BlockSpec(memory_space=pltpu.SMEM)
    vmem = pl.BlockSpec(memory_space=pltpu.VMEM)
    inputs = [
        pltpu.with_memory_space_constraint(x, pltpu.HBM)
        for x in (owner_map.reshape(1, OWNERS), mask, base_scale[0].T, base_codes[0], weights)
    ]
    anywhere = pl.BlockSpec(memory_space=pl.ANY)

    recv, own, scales, codes = pl.pallas_call(
        exchange,
        out_shape=(
            jax.ShapeDtypeStruct((GROUPS * OWNERS, PIECE, BLOCK), jnp.bfloat16),
            jax.ShapeDtypeStruct((1, BLOCK), jnp.int32),
            jax.ShapeDtypeStruct((COL_BLOCKS, ROW_BLOCKS), jnp.float32),
            jax.ShapeDtypeStruct(base_codes.shape[1:], jnp.bfloat16),
        ),
        in_specs=[anywhere] * 5,
        out_specs=(anywhere, vmem, anywhere, anywhere),
        scratch_shapes=[
            pltpu.VMEM((1, OWNERS), jnp.int32),
            pltpu.VMEM(mask.shape, jnp.int32),
            pltpu.VMEM((8, BLOCK), jnp.int32),
            pltpu.SMEM((8, BLOCK), jnp.int32),
            pltpu.VMEM(weights.shape, jnp.bfloat16),
            pltpu.VMEM((COL_BLOCKS, OWNERS, MAIN + 8, BLOCK), jnp.float32),
            pltpu.VMEM((256, 256), jnp.bfloat16),
            pltpu.VMEM((256, BLOCK), jnp.bfloat16),
            pltpu.VMEM((OWNERS, PIECE, BLOCK), jnp.bfloat16),
            pltpu.SemaphoreType.DMA((5,)),
            pltpu.SemaphoreType.DMA((CHUNKS,)),
            pltpu.SemaphoreType.DMA,
            pltpu.SemaphoreType.DMA,
            pltpu.SemaphoreType.DMA,
        ],
        compiler_params=pltpu.CompilerParams(
            collective_id=0, has_side_effects=True, vmem_limit_bytes=32 * 2**20
        ),
        name="exchange",
    )(*inputs)

    deltas, delta_scales = pl.pallas_call(
        decode,
        out_shape=(
            jax.ShapeDtypeStruct(base_codes.shape[1:], jnp.bfloat16),
            jax.ShapeDtypeStruct((COL_BLOCKS, ROW_BLOCKS), jnp.bfloat16),
        ),
        in_specs=[smem, smem, vmem, vmem],
        out_specs=(anywhere, vmem),
        scratch_shapes=[
            pltpu.VMEM((PER_SET * CARRIED, BLOCK, BLOCK), jnp.float32),
            pltpu.VMEM((PER_SET * CARRIED, 8, BLOCK), jnp.float32),
            pltpu.VMEM(base_codes.shape[1:], jnp.bfloat16),
            pltpu.SemaphoreType.DMA,
        ],
        compiler_params=pltpu.CompilerParams(vmem_limit_bytes=24 * 2**20),
        name="decode",
    )(own, scales, recv, codes)
    return deltas[None, None], delta_scales.T[None, None]


def solution(mesh):
    return jax.shard_map(
        body,
        mesh=mesh,
        in_specs=(
            P(None, ("group", "dev"), None),
            P(),
            P(),
            P("dev", None, None),
            P("dev", None, None),
        ),
        out_specs=(P("group", "dev", None, None), P("group", "dev", None, None)),
        check_vma=False,
    )
```

time: 77.4 us -> 62.4 us (0.81)
  local copies, waits for them, and re-layouts: 7.16 us -> 0 us
  Pallas kernels: 66.2 us -> 61.4 us
  between operations: 2.63 us -> 0.64 us
  other arithmetic: 0.85 us -> 0 us
    unnamed x4 -> x0, local copies, waits for them, and re-layouts: 6.56 us -> none
    pallas_call x2, Pallas kernels: 66.2 us -> 61.4 us  [the longest x1 56.5 us: body(): pl.pallas_call(exchange, out_shape=(jax.ShapeDtypeStruct((GROUPS * OWNERS...]
where the time goes in v2:
time: 62.4 us; the launch traced here: 62 us
  Pallas kernels  61.4 us (98%)
  between operations  0.64 us (1%)
    pallas_call x1, Pallas kernels, body(): pl.pallas_call(exchange, out_shape=(jax.ShapeDtypeStruct((GROUPS * OWNERS...  56.5 us
    pallas_call x1, Pallas kernels, body(): pl.pallas_call(decode, out_shape=(jax.ShapeDtypeStruct(base_codes.shape[1...  4.9 us

profile of v2, /device:TPU:0, one launch (start us, length us, event | category | flops | bytes accessed | tf_op | source)
XLA Modules:
  0.0 62.0 jit_solution(10775546332747205038)
XLA Ops:
  0.6 56.5 %exchange.1 = (bf16[128,112,128]{2,1,0:T(8,128)(2,1)S(1)}, s32[1,128]{1,0:T(1,128)S(1)}, f32[8,28]{1,0:T(8,128)S(1)}, bf16[3584,1024]{1,0:T(8,128)(2,1)S(1)}) custom-call(s32[1,64]{1,0:T(1,128)} %bitcast.17, s32[28,8,64]{2,1,0:T(8,128)} %bitcast.15, f32[8,28]{1,0:T(8,128)} %bitcast.16, bf16[3584,1024]{1,0:T(8,128)(2,1)} %bitcast.13, bf16[1792,1024]{1,0:T(8,128)(2,1)} %bitcast.14), custom_call_target="tpu_custom_call" | custom-call | tf_op jit(solution)/shard_map/exchange/pallas_call | solution.py:262
  57.1 4.9 %decode.1 = (bf16[3584,1024]{1,0:T(8,128)(2,1)}, bf16[8,28]{1,0:T(8,128)(2,1)}) custom-call(s32[1,128]{1,0:T(1,128)S(1)} %get-tuple-element.8.own, f32[8,28]{1,0:T(8,128)S(1)} %get-tuple-element.9.scales, bf16[128,112,128]{2,1,0:T(8,128)(2,1)S(1)} %get-tuple-element.10.held, bf16[3584,1024]{1,0:T(8,128)(2,1)S(1)} %get-tuple-element.11.base), custom_call_target="tpu_custom_call" | custom-call | tf_op jit(solution)/shard_map/decode/pallas_call | solution.py:294

commit v3 on v2

--- a/solution.py
+++ b/solution.py
@@ -27,10 +27,10 @@
 def owner_at(me, t):
     core, y, zl, x = me % 2, (me // 2) % 4, (me // 8) % 2, me // 16
     a, b, e = t % 4, (t // 4) % 4, t // 16
-    v = (a + b + e) % 4
+    v = (a + e) % 4
     x = (x + a) % 4
-    y = (y + a + b) % 4
-    zl = (zl + v) % 2
+    y = (y + b + 4 - a) % 4
+    zl = (zl + v % 2) % 2
     core = (core + v // 2) % 2
     return ((x * 2 + zl) * 4 + y) * 2 + core
 
@@ -67,13 +67,6 @@
 
     barrier = pltpu.get_barrier_semaphore()
 
-    def greet(i, carry):
-        other = (my_id + i) % (GROUPS * OWNERS)
-        pl.semaphore_signal(
-            barrier, inc=1, device_id=(other // OWNERS, other % OWNERS), device_id_type=MESH
-        )
-        return carry
-
     def load(i):
         rows = pl.ds(pl.multiple_of(i * CHUNK, CHUNK), CHUNK)
         return pltpu.make_async_copy(weights.at[rows], raw.at[rows], load_sems.at[i])
@@ -86,7 +79,14 @@
     load_masks.start()
     for i in range(CHUNKS):
         load(i).start()
-    lax.fori_loop(1, GROUPS * OWNERS, greet, 0)
+    for other in range(GROUPS * OWNERS):
+
+        @pl.when(other != my_id)
+        def _():
+            pl.semaphore_signal(
+                barrier, inc=1, device_id=(other // OWNERS, other % OWNERS), device_id_type=MESH
+            )
+
     load_scales.start()
     load_codes.start()
 
@@ -169,8 +169,8 @@
 
     def step(t, carry):
         pack(t)
+        to(t, 1 - g).start()
         to(t, g).start()
-        to(t, 1 - g).start()
         return carry
 
     lax.fori_loop(1, OWNERS, step, 0)

time: 62.4 us -> 58.5 us (0.938)
  Pallas kernels: 61.4 us -> 57.7 us
    pallas_call x1, Pallas kernels: 56.5 us -> 52.8 us  [body(): pl.pallas_call(exchange, out_shape=(jax.ShapeDtypeStruct((GROUPS * OWNERS...]
where the time goes in v3:
time: 58.5 us; the launch traced here: 58.3 us
  Pallas kernels  57.7 us (99%)
  between operations  0.64 us (1%)
    pallas_call x1, Pallas kernels, body(): pl.pallas_call(exchange, out_shape=(jax.ShapeDtypeStruct((GROUPS * OWNERS...  52.8 us
    pallas_call x1, Pallas kernels, body(): pl.pallas_call(decode, out_shape=(jax.ShapeDtypeStruct(base_codes.shape[1...  4.89 us

profile of v3, /device:TPU:0, one launch (start us, length us, event | category | flops | bytes accessed | tf_op | source)
XLA Modules:
  0.0 58.3 jit_solution(1319847762187387920)
XLA Ops:
  0.6 52.8 %exchange.1 = (bf16[128,112,128]{2,1,0:T(8,128)(2,1)S(1)}, s32[1,128]{1,0:T(1,128)S(1)}, f32[8,28]{1,0:T(8,128)S(1)}, bf16[3584,1024]{1,0:T(8,128)(2,1)S(1)}) custom-call(s32[1,64]{1,0:T(1,128)} %bitcast.17, s32[28,8,64]{2,1,0:T(8,128)} %bitcast.15, f32[8,28]{1,0:T(8,128)} %bitcast.16, bf16[3584,1024]{1,0:T(8,128)(2,1)} %bitcast.13, bf16[1792,1024]{1,0:T(8,128)(2,1)} %bitcast.14), custom_call_target="tpu_custom_call" | custom-call | tf_op jit(solution)/shard_map/exchange/pallas_call | solution.py:262
  53.4 4.9 %decode.1 = (bf16[3584,1024]{1,0:T(8,128)(2,1)}, bf16[8,28]{1,0:T(8,128)(2,1)}) custom-call(s32[1,128]{1,0:T(1,128)S(1)} %get-tuple-element.8.own, f32[8,28]{1,0:T(8,128)S(1)} %get-tuple-element.9.scales, bf16[128,112,128]{2,1,0:T(8,128)(2,1)S(1)} %get-tuple-element.10.held, bf16[3584,1024]{1,0:T(8,128)(2,1)S(1)} %get-tuple-element.11.base), custom_call_target="tpu_custom_call" | custom-call | tf_op jit(solution)/shard_map/decode/pallas_call | solution.py:294

commit v4 on v3

--- a/solution.py
+++ b/solution.py
@@ -52,9 +52,9 @@
 
 
 def exchange(
-    owner_map, mask, scales, codes, weights, recv, own, scales_out, codes_out,
-    owners, masks, tile, table, raw, by_expert, turn, turn_rest, send,
-    small_sems, load_sems, keep_sem, send_sem, recv_sem,
+    owner_map, mask, scales, codes, weights, recv, own, base, blank,
+    owners, masks, tile, table, own_table, scale_table, raw, by_expert, turn, turn_rest, send, by_column, made, zeros,
+    small_sems, load_sems, code_sems, base_sem, blank_sem, keep_sem, send_sem, recv_sem,
 ):
     g = lax.axis_index("group")
     me = lax.axis_index("dev")
@@ -73,8 +73,11 @@
 
     load_owners = pltpu.make_async_copy(owner_map, owners, small_sems.at[0])
     load_masks = pltpu.make_async_copy(mask, masks, small_sems.at[1])
-    load_scales = pltpu.make_async_copy(scales, scales_out, small_sems.at[2])
-    load_codes = pltpu.make_async_copy(codes, codes_out, small_sems.at[4])
+    load_scales = pltpu.make_async_copy(scales, scale_table, small_sems.at[2])
+    load_codes = [
+        pltpu.make_async_copy(codes.at[:, :, pl.ds(BLOCK * c, BLOCK)], by_column.at[c], code_sems.at[c])
+        for c in range(COL_BLOCKS)
+    ]
     load_owners.start()
     load_masks.start()
     for i in range(CHUNKS):
@@ -88,7 +91,8 @@
             )
 
     load_scales.start()
-    load_codes.start()
+    for copy in load_codes:
+        copy.start()
 
     to_row = lax.broadcasted_iota(jnp.int32, (256, 256), 0)
     from_row = lax.broadcasted_iota(jnp.int32, (256, 256), 1)
@@ -181,15 +185,44 @@
     block = lax.broadcasted_iota(jnp.int32, mine.shape, 0)
     own[...] = jnp.sum(jnp.where(lane == block, mine, 0), axis=0)
 
+    to_own = pltpu.make_async_copy(own, own_table, small_sems.at[4])
+    to_own.start()
+    zeros[...] = jnp.zeros_like(zeros)
+
+    def clear(a):
+        rows = pl.ds(pl.multiple_of(a * BLOCK, BLOCK), BLOCK)
+        return pltpu.make_async_copy(zeros, blank.at[rows], blank_sem)
+
+    def clear_one(a, carry):
+        clear(a).start()
+        return carry
+
+    lax.fori_loop(0, ROW_BLOCKS, clear_one, 0)
     load_scales.wait()
-    load_codes.wait()
+    for copy in load_codes:
+        copy.wait()
+    to_own.wait()
+
+    def base_rows(a, carry):
+        for k in range(CARRIED):
+            col = column_of(own_table[0, a], k)
+            made[a * CARRIED + k] = by_column[col, a].astype(jnp.float32) * scale_table[col, a]
+        return carry
+
+    lax.fori_loop(0, ROW_BLOCKS, base_rows, 0)
+    to_base = pltpu.make_async_copy(made, base, base_sem)
+    to_base.start()
+    to_base.wait()
+    pltpu.make_async_copy(blank, blank, blank_sem).wait()
     keep.wait()
     sent = recv.at[pl.ds(0, PEERS)]
     pltpu.make_async_copy(sent, sent, send_sem).wait()
     pltpu.make_async_copy(sent, sent, recv_sem).wait()
 
 
-def decode(own, scales, held, base, out, out_scales, change, peaks, made, out_sem):
+def decode(own, held, base, blank, out, out_scales, made, change, peaks, table, found_scales, own_sem, scale_sem, out_sem):
+    to_table = pltpu.make_async_copy(own, table, own_sem)
+    to_table.start()
     low = lax.broadcasted_iota(jnp.int32, (8, BLOCK), 0) < 4
     lane = lax.broadcasted_iota(jnp.int32, (COL_BLOCKS, BLOCK), 1)
     column = lax.broadcasted_iota(jnp.int32, (COL_BLOCKS, BLOCK), 0)
@@ -197,15 +230,8 @@
     pairs = per_set // 2
 
     def one_set(s, found):
-        rows_of = [[[] for k in range(CARRIED)] for r in range(PER_SET)]
         for r in range(PER_SET):
             a = s * PER_SET + r
-            here = pl.ds(pl.multiple_of(a * BLOCK, BLOCK), BLOCK)
-            made[here, :] = jnp.zeros((BLOCK, COL_BLOCKS * BLOCK), jnp.bfloat16)
-        for r in range(PER_SET):
-            a = s * PER_SET + r
-            here = pl.ds(pl.multiple_of(a * BLOCK, BLOCK), BLOCK)
-            code = own[0, a]
             first, last = BLOCK * r, BLOCK * (r + 1)
             parts = [[] for k in range(CARRIED)]
             for m in range(first // PAIR, (last + PAIR - 1) // PAIR):
@@ -223,17 +249,17 @@
                     )
                     parts[k].append(whole[max(first - PAIR * m, 0) : min(last - PAIR * m, PAIR)])
             for k in range(CARRIED):
-                col = column_of(code, k)
-                at = pl.ds(pl.multiple_of(col * BLOCK, BLOCK), BLOCK)
-                diff = jnp.concatenate(parts[k], axis=0) - base[here, at].astype(jnp.float32) * scales[col, a]
+                diff = jnp.concatenate(parts[k], axis=0) - base[a * CARRIED + k]
                 change[r * CARRIED + k] = diff
                 peaks[r * CARRIED + k] = jnp.max(jnp.abs(diff).reshape(16, 8, BLOCK), axis=0)
+        if isinstance(s, int) and s == 0:
+            to_table.wait()
         peak = jnp.max(jnp.max(peaks[...], axis=1, keepdims=True), axis=2, keepdims=True) + 1e-06
         inverse = 1.0 / peak
         for r in range(PER_SET):
             a = s * PER_SET + r
             here = pl.ds(pl.multiple_of(a * BLOCK, BLOCK), BLOCK)
-            code = own[0, a]
+            code = table[0, a]
             for k in range(CARRIED):
                 i = r * CARRIED + k
                 col = column_of(code, k)
@@ -243,9 +269,13 @@
             pltpu.make_async_copy(made.at[here], out.at[here], out_sem).start()
         return found
 
-    found = lax.fori_loop(0, SETS, one_set, jnp.zeros((COL_BLOCKS, BLOCK), jnp.float32))
-    out_scales[...] = found[:, :ROW_BLOCKS].astype(jnp.bfloat16)
+    found = one_set(0, jnp.zeros((COL_BLOCKS, BLOCK), jnp.float32))
+    found = lax.fori_loop(1, SETS, one_set, found)
+    found_scales[...] = found[:, :ROW_BLOCKS].astype(jnp.bfloat16)
+    to_scales = pltpu.make_async_copy(found_scales, out_scales, scale_sem)
+    to_scales.start()
     pltpu.make_async_copy(made, out, out_sem).wait()
+    to_scales.wait()
 
 
 def body(new_weights, owner_map, block_mask, base_codes, base_scale):
@@ -253,19 +283,20 @@
     mask = block_mask.transpose(1, 2, 0)
     smem = pl.BlockSpec(memory_space=pltpu.SMEM)
     vmem = pl.BlockSpec(memory_space=pltpu.VMEM)
+    codes = base_codes[0].reshape(ROW_BLOCKS, BLOCK, COL_BLOCKS * BLOCK)
     inputs = [
         pltpu.with_memory_space_constraint(x, pltpu.HBM)
-        for x in (owner_map.reshape(1, OWNERS), mask, base_scale[0].T, base_codes[0], weights)
+        for x in (owner_map.reshape(1, OWNERS), mask, base_scale[0].T, codes, weights)
     ]
     anywhere = pl.BlockSpec(memory_space=pl.ANY)
 
-    recv, own, scales, codes = pl.pallas_call(
+    recv, own, base, blank = pl.pallas_call(
         exchange,
         out_shape=(
-            jax.ShapeDtypeStruct((GROUPS * OWNERS, PIECE, BLOCK), jnp.bfloat16),
-            jax.ShapeDtypeStruct((1, BLOCK), jnp.int32),
-            jax.ShapeDtypeStruct((COL_BLOCKS, ROW_BLOCKS), jnp.float32),
-            jax.ShapeDtypeStruct(base_codes.shape[1:], jnp.bfloat16),
+            pltpu.VMEM((GROUPS * OWNERS, PIECE, BLOCK), jnp.bfloat16),
+            pltpu.VMEM((1, BLOCK), jnp.int32),
+            pltpu.VMEM((ROW_BLOCKS * CARRIED, BLOCK, BLOCK), jnp.float32),
+            pltpu.VMEM(base_codes.shape[1:], jnp.bfloat16),
         ),
         in_specs=[anywhere] * 5,
         out_specs=(anywhere, vmem, anywhere, anywhere),
@@ -274,40 +305,53 @@
             pltpu.VMEM(mask.shape, jnp.int32),
             pltpu.VMEM((8, BLOCK), jnp.int32),
             pltpu.SMEM((8, BLOCK), jnp.int32),
+            pltpu.SMEM((1, BLOCK), jnp.int32),
+            pltpu.SMEM((COL_BLOCKS, ROW_BLOCKS), jnp.float32),
             pltpu.VMEM(weights.shape, jnp.bfloat16),
             pltpu.VMEM((COL_BLOCKS, OWNERS, MAIN + 8, BLOCK), jnp.float32),
             pltpu.VMEM((256, 256), jnp.bfloat16),
             pltpu.VMEM((256, BLOCK), jnp.bfloat16),
             pltpu.VMEM((OWNERS, PIECE, BLOCK), jnp.bfloat16),
+            pltpu.VMEM((COL_BLOCKS, ROW_BLOCKS, BLOCK, BLOCK), jnp.bfloat16),
+            pltpu.VMEM((ROW_BLOCKS * CARRIED, BLOCK, BLOCK), jnp.float32),
+            pltpu.VMEM((BLOCK, COL_BLOCKS * BLOCK), jnp.bfloat16),
             pltpu.SemaphoreType.DMA((5,)),
             pltpu.SemaphoreType.DMA((CHUNKS,)),
+            pltpu.SemaphoreType.DMA((COL_BLOCKS,)),
+            pltpu.SemaphoreType.DMA,
+            pltpu.SemaphoreType.DMA,
             pltpu.SemaphoreType.DMA,
             pltpu.SemaphoreType.DMA,
             pltpu.SemaphoreType.DMA,
         ],
         compiler_params=pltpu.CompilerParams(
-            collective_id=0, has_side_effects=True, vmem_limit_bytes=32 * 2**20
+            collective_id=0, has_side_effects=True, vmem_limit_bytes=40 * 2**20
         ),
         name="exchange",
     )(*inputs)
 
-    deltas, delta_scales = pl.pallas_call(
+    deltas, delta_scales, _ = pl.pallas_call(
         decode,
         out_shape=(
             jax.ShapeDtypeStruct(base_codes.shape[1:], jnp.bfloat16),
             jax.ShapeDtypeStruct((COL_BLOCKS, ROW_BLOCKS), jnp.bfloat16),
+            pltpu.VMEM(base_codes.shape[1:], jnp.bfloat16),
         ),
-        in_specs=[smem, smem, vmem, vmem],
-        out_specs=(anywhere, vmem),
+        in_specs=[anywhere, vmem, vmem, vmem],
+        out_specs=(anywhere, anywhere, vmem),
+        input_output_aliases={3: 2},
         scratch_shapes=[
             pltpu.VMEM((PER_SET * CARRIED, BLOCK, BLOCK), jnp.float32),
             pltpu.VMEM((PER_SET * CARRIED, 8, BLOCK), jnp.float32),
-            pltpu.VMEM(base_codes.shape[1:], jnp.bfloat16),
+            pltpu.SMEM((1, BLOCK), jnp.int32),
+            pltpu.VMEM((COL_BLOCKS, ROW_BLOCKS), jnp.bfloat16),
+            pltpu.SemaphoreType.DMA,
+            pltpu.SemaphoreType.DMA,
             pltpu.SemaphoreType.DMA,
         ],
         compiler_params=pltpu.CompilerParams(vmem_limit_bytes=24 * 2**20),
         name="decode",
-    )(own, scales, recv, codes)
+    )(*(pltpu.with_memory_space_constraint(x, pltpu.VMEM) for x in (own, recv, base, blank)))
     return deltas[None, None], delta_scales.T[None, None]
 
 

time: 58.5 us -> 57.3 us (0.979)
  Pallas kernels: 57.7 us -> 56.5 us
    pallas_call x1, Pallas kernels: 4.89 us -> 3.64 us  [body(): pl.pallas_call(decode, out_shape=(jax.ShapeDtypeStruct(base_codes.shape[1...]
where the time goes in v4:
time: 57.3 us; the launch traced here: 57.2 us
  Pallas kernels  56.5 us (99%)
  between operations  0.64 us (1%)
    pallas_call x1, Pallas kernels, body(): pl.pallas_call(exchange, out_shape=(pltpu.VMEM((GROUPS * OWNERS, PIECE, B...  52.9 us
    pallas_call x1, Pallas kernels, body(): pl.pallas_call(decode, out_shape=(jax.ShapeDtypeStruct(base_codes.shape[1...  3.64 us

profile of v4, /device:TPU:0, one launch (start us, length us, event | category | flops | bytes accessed | tf_op | source)
XLA Modules:
  0.0 57.2 jit_solution(15013765935671333144)
XLA Ops:
  0.6 52.9 %exchange.1 = (bf16[128,112,128]{2,1,0:T(8,128)(2,1)S(1)}, s32[1,128]{1,0:T(1,128)S(1)}, f32[112,128,128]{2,1,0:T(8,128)S(1)}, bf16[3584,1024]{1,0:T(8,128)(2,1)S(1)}) custom-call(s32[1,64]{1,0:T(1,128)} %bitcast.17, s32[28,8,64]{2,1,0:T(8,128)} %bitcast.15, f32[8,28]{1,0:T(8,128)} %bitcast.16, bf16[28,128,1024]{2,1,0:T(8,128)(2,1)} %bitcast.13, ...), custom_call_target="tpu_custom_call" | custom-call | tf_op jit(solution)/shard_map/exchange/pallas_call | solution.py:293
  53.5 3.6 %decode.1 = (bf16[3584,1024]{1,0:T(8,128)(2,1)}, bf16[8,28]{1,0:T(8,128)(2,1)}, bf16[3584,1024]{1,0:T(8,128)(2,1)S(1)}) custom-call(s32[1,128]{1,0:T(1,128)S(1)} %get-tuple-element.8.own, bf16[128,112,128]{2,1,0:T(8,128)(2,1)S(1)} %get-tuple-element.9.held, f32[112,128,128]{2,1,0:T(8,128)S(1)} %get-tuple-element.10.base, ...), custom_call_target="tpu_custom_call", output_to_operand_aliasing={{2}: (3, {})} | custom-call | tf_op jit(solution)/shard_map/decode/pallas_call | solution.py:333

commit v5 on v4

--- a/solution.py
+++ b/solution.py
@@ -220,7 +220,7 @@
     pltpu.make_async_copy(sent, sent, recv_sem).wait()
 
 
-def decode(own, held, base, blank, out, out_scales, made, change, peaks, table, found_scales, own_sem, scale_sem, out_sem):
+def decode(own, held, base, blank, out, out_scales, made, change, peaks, table, own_sem, out_sem):
     to_table = pltpu.make_async_copy(own, table, own_sem)
     to_table.start()
     low = lax.broadcasted_iota(jnp.int32, (8, BLOCK), 0) < 4
@@ -271,11 +271,8 @@
 
     found = one_set(0, jnp.zeros((COL_BLOCKS, BLOCK), jnp.float32))
     found = lax.fori_loop(1, SETS, one_set, found)
-    found_scales[...] = found[:, :ROW_BLOCKS].astype(jnp.bfloat16)
-    to_scales = pltpu.make_async_copy(found_scales, out_scales, scale_sem)
-    to_scales.start()
+    out_scales[...] = found[:, :ROW_BLOCKS].astype(jnp.bfloat16)
     pltpu.make_async_copy(made, out, out_sem).wait()
-    to_scales.wait()
 
 
 def body(new_weights, owner_map, block_mask, base_codes, base_scale):
@@ -338,14 +335,12 @@
             pltpu.VMEM(base_codes.shape[1:], jnp.bfloat16),
         ),
         in_specs=[anywhere, vmem, vmem, vmem],
-        out_specs=(anywhere, anywhere, vmem),
+        out_specs=(anywhere, vmem, vmem),
         input_output_aliases={3: 2},
         scratch_shapes=[
             pltpu.VMEM((PER_SET * CARRIED, BLOCK, BLOCK), jnp.float32),
             pltpu.VMEM((PER_SET * CARRIED, 8, BLOCK), jnp.float32),
             pltpu.SMEM((1, BLOCK), jnp.int32),
-            pltpu.VMEM((COL_BLOCKS, ROW_BLOCKS), jnp.bfloat16),
-            pltpu.SemaphoreType.DMA,
             pltpu.SemaphoreType.DMA,
             pltpu.SemaphoreType.DMA,
         ],

time: 57.3 us -> 57.9 us (1.010)
  Pallas kernels: 56.5 us -> 57.1 us
where the time goes in v5:
time: 57.9 us; the launch traced here: 57.7 us
  Pallas kernels  57.1 us (99%)
  between operations  0.64 us (1%)
    pallas_call x1, Pallas kernels, body(): pl.pallas_call(exchange, out_shape=(pltpu.VMEM((GROUPS * OWNERS, PIECE, B...  52.9 us
    pallas_call x1, Pallas kernels, body(): pl.pallas_call(decode, out_shape=(jax.ShapeDtypeStruct(base_codes.shape[1...  4.2 us

profile of v5, /device:TPU:0, one launch (start us, length us, event | category | flops | bytes accessed | tf_op | source)
XLA Modules:
  0.0 57.7 jit_solution(10521067661068534304)
XLA Ops:
  0.6 52.9 %exchange.1 = (bf16[128,112,128]{2,1,0:T(8,128)(2,1)S(1)}, s32[1,128]{1,0:T(1,128)S(1)}, f32[112,128,128]{2,1,0:T(8,128)S(1)}, bf16[3584,1024]{1,0:T(8,128)(2,1)S(1)}) custom-call(s32[1,64]{1,0:T(1,128)} %bitcast.17, s32[28,8,64]{2,1,0:T(8,128)} %bitcast.15, f32[8,28]{1,0:T(8,128)} %bitcast.16, bf16[28,128,1024]{2,1,0:T(8,128)(2,1)} %bitcast.13, ...), custom_call_target="tpu_custom_call" | custom-call | tf_op jit(solution)/shard_map/exchange/pallas_call | solution.py:290
  53.5 4.2 %decode.1 = (bf16[3584,1024]{1,0:T(8,128)(2,1)}, bf16[8,28]{1,0:T(8,128)(2,1)}, bf16[3584,1024]{1,0:T(8,128)(2,1)S(1)}) custom-call(s32[1,128]{1,0:T(1,128)S(1)} %get-tuple-element.8.own, bf16[128,112,128]{2,1,0:T(8,128)(2,1)S(1)} %get-tuple-element.9.held, f32[112,128,128]{2,1,0:T(8,128)S(1)} %get-tuple-element.10.base, ...), custom_call_target="tpu_custom_call", output_to_operand_aliasing={{2}: (3, {})} | custom-call | tf_op jit(solution)/shard_map/decode/pallas_call | solution.py:330
